TPU v7x, 32 devices: a whole 2x2x4 slice. The times are simulated.
32 devices in a mesh: groups: 2 (over x), expert: 8 (over z, y), cuts: 2 (over core).
Axes of the slice: x: 2, y: 2, z: 4, core: 2. Of those that a mesh axis runs over, the one named last changes fastest.
Arguments:
- tokens: bfloat16 [512, 3584], P(('groups', 'expert', 'cuts')), parts along dimension 0, may hold values from -6 to 6
- expert_ids: int32 [512, 2], P(('groups', 'expert', 'cuts')), parts along dimension 0, may hold values from 0 to 1, as said below
- route_weights: float32 [512, 2], P(('groups', 'expert', 'cuts')), parts along dimension 0, may hold values from 0.2 to 1
- gate_weight: bfloat16 [3584, 6144], P(None, ('expert', 'cuts')), may hold values from -0.09375 to 0.09375
- up_weight: bfloat16 [3584, 6144], P(None, ('expert', 'cuts')), may hold values from -0.09375 to 0.09375
- down_weight: bfloat16 [3584, 6144], P(None, ('expert', 'cuts')), may hold values from -0.109375 to 0.109375
Outputs:
- moe_output: bfloat16 [512, 3584], P(('groups', 'expert', 'cuts')), parts along dimension 0
There are 2 independent parts, one for each index of `groups`. A program takes and returns all parts, laid end to end along the dimension named above; an argument that names none is the same for every part. Nothing has to cross between parts.
Inputs may be any that keep to these rules, and one draw needn't show every extreme that they name: `expert_ids`: each row names two different experts. Within each device's aligned block of 16 rows no expert is named more than 16 times, and in every draw one expert is named exactly 16 times in every block.
All inputs are finite; a program needn't handle non-finite values.
Results may differ from a plain program's by a relative error of at most 0.0057.
Values may be sent and summed in bfloat16 or wider, within the bound.
A program may use at most 64 MiB of HBM per device.

v0:
```python
import jax
import jax.numpy as jnp
from jax import lax
from jax.sharding import PartitionSpec as P

SPREAD = 4


def swapped(block, axis, distance):
    count = lax.axis_size(axis)
    route = []
    for low in range(count):
        high = low | 1 << distance
        if high != low and high < count:
            route += [(low, high), (high, low)]
    return lax.ppermute(block, axis, route)


def hidden_part(block_rows, w_gate, w_up):
    gate_proj = jnp.dot(block_rows, w_gate, preferred_element_type=jnp.float32)
    up_proj = jnp.dot(block_rows, w_up, preferred_element_type=jnp.float32)
    return (jax.nn.silu(gate_proj) * up_proj).astype(jnp.bfloat16)


def expert_part(block_rows, w_gate, w_up, w_down):
    hidden = hidden_part(block_rows, w_gate, w_up)
    return lax.dot_general(
        hidden, w_down, (((1,), (1,)), ((), ())), preferred_element_type=jnp.float32
    )


def per_device(tokens, expert_ids, route_weights, gate_weight, up_weight, down_weight):
    tok_rows, feat_width = tokens.shape
    n_expert = lax.axis_size("expert")
    experts = n_expert // SPREAD
    capacity = min(tok_rows, 2 * ((2 * tok_rows + experts - 1) // experts))
    quarter = feat_width // SPREAD
    my_index = lax.axis_index("expert")
    flat_ids = expert_ids.reshape(-1)
    onehot = (flat_ids[:, None] == jnp.arange(experts, dtype=jnp.int32)[None, :]).astype(jnp.int32)
    earlier = jnp.cumsum(onehot, axis=0) - onehot
    slot_ids = jnp.sum(earlier * onehot, axis=1).reshape(tok_rows, 2)
    targets = expert_ids * capacity + slot_ids
    columns = jnp.arange(experts * capacity, dtype=jnp.int32)
    placing = jnp.any(targets[None, :, :] == columns[:, None, None], axis=2).astype(jnp.bfloat16)
    outgoing = jnp.dot(placing, tokens, preferred_element_type=jnp.float32).astype(jnp.bfloat16)
    outgoing = outgoing.reshape(experts, capacity, feat_width)
    copies = jnp.repeat(outgoing, SPREAD, axis=0)
    arrived = lax.all_to_all(copies, "expert", split_axis=0, concat_axis=0, tiled=True)
    row_piece = lax.all_gather(arrived, "cuts", axis=0, tiled=True)
    piece_rows = row_piece.reshape(-1, feat_width)
    result_rows = expert_part(piece_rows, gate_weight, up_weight, down_weight)
    partial_terms = result_rows.reshape(row_piece.shape)
    partial_value = lax.psum_scatter(
        partial_terms, "cuts", scatter_dimension=0, tiled=True
    ).reshape(n_expert * capacity, feat_width)
    summed = partial_value
    for bit_level in (1, 0):
        half_width = summed.shape[1] // 2
        upper_half = my_index >> bit_level & 1 == 1
        lower_part = summed[:, :half_width]
        upper_part = summed[:, half_width:]
        kept_part = jnp.where(upper_half, upper_part, lower_part)
        given_part = jnp.where(upper_half, lower_part, upper_part)
        summed = kept_part + swapped(given_part, "expert", bit_level)
    expert_rows = summed.astype(jnp.bfloat16).reshape(n_expert, capacity, quarter)
    returned = lax.all_to_all(expert_rows, "expert", split_axis=0, concat_axis=0, tiled=True)
    results = returned.reshape(experts, SPREAD, capacity, quarter).transpose(0, 2, 1, 3)
    results = results.reshape(experts * capacity, feat_width)
    weighting = jnp.sum(
        jnp.where(targets[:, :, None] == columns[None, None, :], route_weights[:, :, None], 0.0),
        axis=1,
    )
    mixed_rows = jnp.dot(
        weighting,
        results.astype(jnp.float32),
        precision=lax.Precision.HIGHEST,
        preferred_element_type=jnp.float32,
    )
    return mixed_rows.astype(jnp.bfloat16)


def solution(mesh):
    in_specs = (
        P(("groups", "expert", "cuts"), None),
        P(("groups", "expert", "cuts"), None),
        P(("groups", "expert", "cuts"), None),
        P(None, ("expert", "cuts")),
        P(None, ("expert", "cuts")),
        P(None, ("expert", "cuts")),
    )
    out_specs = P(("groups", "expert", "cuts"), None)
    return jax.shard_map(
        per_device, mesh=mesh, in_specs=in_specs, out_specs=out_specs, check_vma=False
    )
```

profile of v0, /device:TPU:0, one launch (start us, length us, event | category | flops | bytes accessed | tf_op | source)
XLA Modules:
  0.0 133.9 jit_solution(1083497235979108337)
XLA Ops:
  6.5 0.0 copy-start
  6.5 0.0 all-gather.2.cloned.1.call-start
  6.5 0.9 copy.31
  7.4 0.1 eq.47
  7.5 0.1 fusion.8
  7.6 0.1 reduce_window_sum.11
  7.7 0.2 select_reduce_fusion.1
  7.8 0.1 reshape.31
  7.9 0.1 copy.32
  8.0 0.7 multiply_add_fusion
  8.7 0.1 fusion.9
  8.8 1.2 convolution_convert_fusion
  10.0 0.1 broadcast_in_dim.23
  10.0 30.5 %all_to_all.10 = bf16[8,16,3584]{2,1,0:T(8,128)(2,1)} all-to-all(bf16[8,16,3584]{2,1,0:T(8,128)(2,1)S(1)} %bitcast.24), channel_id=1, replica_groups=mesh['groups'=2,'expert'=8,'cuts'=2] {'expert'}, dimensions={0} | all-to-all | bytes 1835008 | tf_op jit(solution)/shard_map/all_to_all | solution.py:49
  40.5 0.0 all-gather.2.cloned.1.call-update
  40.6 0.0 reduce-scatter.2.cloned.1.call-start
  40.6 8.9 %all-gather.2.cloned.1.call-done = bf16[16,16,3584]{2,1,0:T(8,128)(2,1)} async-done(((bf16[8,16,3584]{2,1,0:T(8,128)(2,1)}), bf16[16,16,3584]{2,1,0:T(8,128)(2,1)}) %all-gather.2.cloned.1.call-update) | async-done | bytes 1835024 | tf_op jit(solution)/shard_map/all_gather | solution.py:50
  49.5 3.5 %fusion.11 = f32[256,384]{1,0:T(8,128)S(1)} fusion(bf16[256,3584]{1,0:T(8,128)(2,1)} %bitcast.25, bf16[3584,384]{1,0:T(8,128)(2,1)} %param.9), kind=kOutput, calls=%fused_computation.24 | convolution fusion | flops 704643072 | bytes 4980736 | tf_op jit(solution)/shard_map/dot_general | solution.py:20
  53.0 0.0 copy-done
  53.0 6.3 %fusion.1 = f32[256,3584]{1,0:T(8,128)} fusion(bf16[3584,384]{1,0:T(8,128)(2,1)S(1)} %copy-done, bf16[256,3584]{1,0:T(8,128)(2,1)} %bitcast.26, bf16[3584,384]{1,0:T(8,128)(2,1)} %param.10, f32[256,384]{1,0:T(8,128)S(1)} %fusion.11), kind=kOutput, calls=%fused_computation.4 | convolution fusion | flops 1409875968 | bytes 11403264 | tf_op jit(solution)/shard_map/dot_general | solution.py:27
  59.3 0.0 reduce-scatter.2.cloned.1.call-update
  59.4 12.9 %reduce-scatter.2.cloned.1.call-done = f32[8,16,3584]{2,1,0:T(8,128)} async-done(((f32[16,16,3584]{2,1,0:T(8,128)}), f32[8,16,3584]{2,1,0:T(8,128)}) %reduce-scatter.2.cloned.1.call-update) | async-done | bytes 1835024 | tf_op jit(solution)/shard_map/reduce_scatter | solution.py:54
  72.2 2.5 %slice_select_fusion = f32[128,1792]{1,0:T(8,128)} fusion(f32[128,3584]{1,0:T(8,128)} %bitcast.22, pred[]{:T(512)S(6)} %eq.55), kind=kLoop, calls=%fused_computation.6 | loop fusion | flops 229376 | bytes 2752513 | tf_op jit(solution)/shard_map/jit(_where)/select_n | solution.py:64
  74.7 1.7 %collective-permute-start = (f32[128,1792]{1,0:T(8,128)}, f32[128,1792]{1,0:T(8,128)}, u32[]{:S(2)}, u32[]{:S(2)}) collective-permute-start(f32[128,1792]{1,0:T(8,128)} %slice_select_fusion), channel_id=1, source_target_pairs={{0,4},{4,0},{2,6},{6,2},{8,12},{12,8},{10,14},{14,10},{1,5},{5,1},... | collective-permute-start | bytes 2752520 | tf_op jit(solution)/shard_map/ppermute | solution.py:16
  76.5 0.0 copy-start.1
  76.5 21.2 %collective-permute-done = f32[128,1792]{1,0:T(8,128)} collective-permute-done((f32[128,1792]{1,0:T(8,128)}, f32[128,1792]{1,0:T(8,128)}, u32[]{:S(2)}, u32[]{:S(2)}) %collective-permute-start) | collective-permute-done | bytes 917536 | tf_op jit(solution)/shard_map/ppermute | solution.py:16
  97.6 1.9 %select_add_fusion = f32[128,1792]{1,0:T(8,128)S(1)} fusion(f32[128,1792]{1,0:T(8,128)} %collective-permute-done, f32[128,3584]{1,0:T(8,128)} %bitcast.23, pred[]{:T(512)S(6)} %eq.55), kind=kLoop, calls=%fused_computation.5 | loop fusion | flops 458752 | bytes 3670017 | tf_op jit(solution)/shard_map/add | solution.py:65
  99.5 1.8 %collective-permute-start.1 = (f32[128,896]{1,0:T(8,128)S(1)}, f32[128,896]{1,0:T(8,128)S(1)}, u32[]{:S(2)}, u32[]{:S(2)}) collective-permute-start(f32[128,896]{1,0:T(8,128)S(1)} %slice_select_fusion.1), channel_id=1, source_target_pairs={{0,2},{2,0},{4,6},{6,4},{8,10},{10,8},{12,14},{14,12},{1,3},{3,1},... | collective-permute-start | bytes 1376264 | tf_op jit(solution)/shard_map/ppermute | solution.py:16
  101.3 10.2 %collective-permute-done.1 = f32[128,896]{1,0:T(8,128)S(1)} collective-permute-done((f32[128,896]{1,0:T(8,128)S(1)}, f32[128,896]{1,0:T(8,128)S(1)}, u32[]{:S(2)}, u32[]{:S(2)}) %collective-permute-start.1) | collective-permute-done | bytes 458784 | tf_op jit(solution)/shard_map/ppermute | solution.py:16
  111.5 0.8 add_convert_fusion
  112.3 5.8 %all-to-all-start.1 = ((bf16[8,16,896]{2,1,0:T(8,128)(2,1)}), bf16[8,16,896]{2,1,0:T(8,128)(2,1)S(1)}, u32[]{:S(2)}, u32[]{:S(2)}) async-start(bf16[8,16,896]{2,1,0:T(8,128)(2,1)} %bitcast.5), calls=%async_computation.2 | async-start | bytes 458752 | tf_op jit(solution)/shard_map/all_to_all | solution.py:67
  118.1 0.0 copy-done.1
  118.1 0.1 select_reduce_fusion
  118.2 7.9 %all-to-all-done.1 = bf16[8,16,896]{2,1,0:T(8,128)(2,1)S(1)} async-done(((bf16[8,16,896]{2,1,0:T(8,128)(2,1)}), bf16[8,16,896]{2,1,0:T(8,128)(2,1)S(1)}, u32[]{:S(2)}, u32[]{:S(2)}) %all-to-all-start.1) | async-done | bytes 229408 | tf_op jit(solution)/shard_map/all_to_all | solution.py:67
  126.1 0.1 copy.33
  126.2 0.9 convolution_convert_fusion.1
  (2 shorter events, 0.1 us)
Async XLA Ops:
  6.5 46.5 %copy-start = (bf16[3584,384]{1,0:T(8,128)(2,1)S(1)}, bf16[3584,384]{1,0:T(8,128)(2,1)}, u32[]{:S(2)}) copy-start(bf16[3584,384]{1,0:T(8,128)(2,1)} %param.11) | copy-start | bytes 8257540
  6.5 43.0 %all-gather.2.cloned.1.call-start = ((), (), s32[]{:S(2)}) async-start(), calls=%async_computation.3 | async-start | bytes 2752512 | tf_op jit(solution)/shard_map/all_gather | solution.py:50
  40.6 31.7 %reduce-scatter.2.cloned.1.call-start = ((), (), s32[]{:S(2)}) async-start(), calls=%async_computation.4 | async-start | bytes 5505024 | tf_op jit(solution)/shard_map/reduce_scatter | solution.py:54
  74.7 22.9 %collective-permute-start = (f32[128,1792]{1,0:T(8,128)}, f32[128,1792]{1,0:T(8,128)}, u32[]{:S(2)}, u32[]{:S(2)}) collective-permute-start(f32[128,1792]{1,0:T(8,128)} %slice_select_fusion), channel_id=1, source_target_pairs={{0,4},{4,0},{2,6},{6,2},{8,12},{12,8},{10,14},{14,10},{1,5},{5,1},... | collective-permute-start | bytes 2752520 | tf_op jit(solution)/shard_map/ppermute | solution.py:16
  76.5 41.6 %copy-start.1 = (f32[16,2]{0,1:T(2,128)S(1)}, f32[16,2]{0,1:T(2,128)}, u32[]{:S(2)}) copy-start(f32[16,2]{0,1:T(2,128)} %param.8) | copy-start | bytes 388
  99.5 12.0 %collective-permute-start.1 = (f32[128,896]{1,0:T(8,128)S(1)}, f32[128,896]{1,0:T(8,128)S(1)}, u32[]{:S(2)}, u32[]{:S(2)}) collective-permute-start(f32[128,896]{1,0:T(8,128)S(1)} %slice_select_fusion.1), channel_id=1, source_target_pairs={{0,2},{2,0},{4,6},{6,4},{8,10},{10,8},{12,14},{14,12},{1,3},{3,1},... | collective-permute-start | bytes 1376264 | tf_op jit(solution)/shard_map/ppermute | solution.py:16
  112.3 13.8 %all-to-all-start.1 = ((bf16[8,16,896]{2,1,0:T(8,128)(2,1)}), bf16[8,16,896]{2,1,0:T(8,128)(2,1)S(1)}, u32[]{:S(2)}, u32[]{:S(2)}) async-start(bf16[8,16,896]{2,1,0:T(8,128)(2,1)} %bitcast.5), calls=%async_computation.2 | async-start | bytes 458752 | tf_op jit(solution)/shard_map/all_to_all | solution.py:67
Sparse Core Ops, SparseCore 0:
  40.7 8.8 all-gather.1
  59.5 12.7 reduce-scatter.1
where the time goes:
time: 134 us
  waiting for transfers between devices  61.1 us (46%)
  blocking collectives  30.5 us (23%)
  between operations  13.5 us (10%)
  matrix products  11.8 us (9%)
  starting transfers between devices  9.33 us (7%)
  other arithmetic  6.37 us (5%)
  local copies, waits for them, and re-layouts  1.35 us (1%)
    ppermute x2, waiting for transfers between devices, swapped(): return lax.ppermute(block, axis, route)  31.4 us
    all_to_all x1, blocking collectives, per_device(): lax.all_to_all(copies, 'expert', split_axis=0, concat_axis=0, tiled=True)  30.5 us
    reduce_scatter x1, waiting for transfers between devices, per_device(): lax.psum_scatter(partial_terms, 'cuts', scatter_dimension=0, tiled=True)  12.9 us
    all_gather x1, waiting for transfers between devices, per_device(): row_piece = lax.all_gather(arrived, 'cuts', axis=0, tiled=True)  8.93 us
    all_to_all x1, waiting for transfers between devices, per_device(): lax.all_to_all(expert_rows, 'expert', split_axis=0, concat_axis=0, tiled=...  7.92 us
    dot_general x1, matrix products, expert_part(): lax.dot_general(hidden, w_down, (((1,), (1,)), ((), ())), preferred_eleme...  6.29 us
    all_to_all x1, starting transfers between devices, per_device(): lax.all_to_all(expert_rows, 'expert', split_axis=0, concat_axis=0, tiled=...  5.78 us
    ppermute x2, starting transfers between devices, swapped(): return lax.ppermute(block, axis, route)  3.51 us
  transfers between devices with their start and end apart: 5, of which 5 were waited for; matrix products, arithmetic and copies ran while one was open for 0% of the time, Pallas kernels for 0%

commit v1 on v0

--- a/solution.py
+++ b/solution.py
@@ -1,6 +1,10 @@
+import functools
+
 import jax
 import jax.numpy as jnp
 from jax import lax
+from jax.experimental import pallas as pl
+from jax.experimental.pallas import tpu as pltpu
 from jax.sharding import PartitionSpec as P
 
 SPREAD = 4
@@ -80,6 +84,238 @@
     return mixed_rows.astype(jnp.bfloat16)
 
 
+CHOICES = 2
+LANES = 128
+CORE_LAG, PAIR_LAG, LINE_LAG = 1, 3, 5
+
+
+def chunk_width(feat_width):
+    for width in (512, 256, 128):
+        if feat_width % width == 0:
+            return width
+    return feat_width
+
+
+def dense_kernel(
+    experts, tok, ids, mix, w_gate, w_up, w_down, out,
+    gate_v, up_v, down_v, rows, scale, gate_acc, up_acc,
+    kept_core, core_out, core_in, kept_pair, pair_out, pair_in, kept_line, line_out, line_in,
+    w_sem, own_sem, g_send, g_recv, s_send, s_recv, r_send, r_recv,
+):
+    chunks, _, _, line, height, width = rows.shape
+    n_expert = lax.axis_size("expert")
+    place, core = lax.axis_index("expert"), lax.axis_index("cuts")
+    along, side = place // 2, place % 2
+    core_peer = {"cuts": 1 - core}
+    pair_peer = {"expert": along * 2 + 1 - side}
+    line_peers = [{"expert": lax.rem(along + step, line) * 2 + side} for step in range(1, line)]
+    peers = [core_peer, pair_peer] + line_peers
+    my_expert = place // (n_expert // experts)
+
+    loads = [
+        pltpu.make_async_copy(source, target, w_sem.at[at])
+        for at, (source, target) in enumerate(((w_gate, gate_v), (w_up, up_v), (w_down, down_v)))
+    ]
+    own = [
+        pltpu.make_async_copy(tok.at[:, pl.ds(j * width, width)], rows.at[j, 0, 0, 0], own_sem.at[j])
+        for j in range(chunks)
+    ]
+    for copy in own + loads:
+        copy.start()
+    lane = lax.broadcasted_iota(jnp.int32, (height, LANES), 1)
+    own_scale = jnp.zeros((height, LANES), jnp.float32)
+    for k in range(CHOICES):
+        own_scale += jnp.where(lane == ids[:, k:k + 1], mix[:, k:k + 1], 0.0)
+    scale[0, 0, 0] = own_scale
+
+    barrier = pltpu.get_barrier_semaphore()
+    for peer in peers:
+        pl.semaphore_signal(barrier, inc=1, device_id=peer, device_id_type=pl.DeviceIdType.MESH)
+    pl.semaphore_wait(barrier, len(peers))
+
+    def send(source, target, send_sem, recv_sem, peer):
+        copy = pltpu.make_async_remote_copy(
+            src_ref=source, dst_ref=target, send_sem=send_sem, recv_sem=recv_sem,
+            device_id=peer, device_id_type=pl.DeviceIdType.MESH,
+        )
+        copy.start()
+        return copy
+
+    sent = {}
+    for j in range(chunks):
+        mine = tok.at[:, pl.ds(j * width, width)]
+        for step in range(1, line):
+            sent[j, step] = send(
+                mine, rows.at[j, 0, 0, line - step], g_send.at[j, step], g_recv.at[j, line - step],
+                line_peers[step - 1],
+            )
+        sent[j, "pair own"] = send(
+            mine, rows.at[j, 0, 1, 0], g_send.at[j, line], g_recv.at[j, line], pair_peer
+        )
+    for step in range(1, line):
+        sent["s", step] = send(
+            scale.at[0, 0, 0], scale.at[0, 0, line - step], s_send.at[step], s_recv.at[line - step],
+            line_peers[step - 1],
+        )
+
+    for turn in range(chunks + 2):
+        if turn < chunks:
+            j = turn
+            for step in range(1, line):
+                sent[j, line - step].wait_recv()
+            sent[j, "pair"] = send(
+                rows.at[j, 0, 0, pl.ds(1, line - 1)], rows.at[j, 0, 1, pl.ds(1, line - 1)],
+                g_send.at[j, line + 1], g_recv.at[j, line + 1], pair_peer,
+            )
+            own[j].wait()
+            sent[j, "core"] = send(
+                rows.at[j, 0, 0], rows.at[j, 1, 0],
+                g_send.at[j, line + 2], g_recv.at[j, line + 2], core_peer,
+            )
+        if turn == chunks - 1:
+            for step in range(1, line):
+                sent["s", line - step].wait_recv()
+            sent["s", "pair"] = send(
+                scale.at[0, 0], scale.at[0, 1], s_send.at[line], s_recv.at[line], pair_peer
+            )
+        if 1 <= turn <= chunks:
+            j = turn - 1
+            sent[j, "pair own"].wait_recv()
+            sent[j, "pair"].wait_recv()
+            sent[j, "core pair"] = send(
+                rows.at[j, 0, 1], rows.at[j, 1, 1],
+                g_send.at[j, line + 3], g_recv.at[j, line + 3], core_peer,
+            )
+        if turn == chunks:
+            sent["s", "pair"].wait_recv()
+            sent["s", "core"] = send(
+                scale.at[0], scale.at[1], s_send.at[line + 1], s_recv.at[line + 1], core_peer
+            )
+        if turn >= 2:
+            j = turn - 2
+            sent[j, "core"].wait_recv()
+            sent[j, "core pair"].wait_recv()
+            if j == 0:
+                loads[0].wait()
+                loads[1].wait()
+            block = rows[j].reshape(-1, width)
+            depth = pl.ds(j * width, width)
+            gate_part = jnp.dot(block, gate_v[depth, :], preferred_element_type=jnp.float32)
+            up_part = jnp.dot(block, up_v[depth, :], preferred_element_type=jnp.float32)
+            if j == 0:
+                gate_acc[...] = gate_part
+                up_acc[...] = up_part
+            else:
+                gate_acc[...] += gate_part
+                up_acc[...] += up_part
+
+    gate = gate_acc[...]
+    hidden = (gate / (1.0 + jnp.exp(-gate)) * up_acc[...]).astype(jnp.bfloat16)
+    sent["s", "core"].wait_recv()
+    weights = scale[...].reshape(-1, LANES)
+    lane = lax.broadcasted_iota(jnp.int32, weights.shape, 1)
+    weight = jnp.sum(jnp.where(lane == my_expert, weights, 0.0), axis=1, keepdims=True)
+    loads[2].wait()
+
+    pair_rows, line_rows = 2 * line * height, line * height
+    back = {}
+    for turn in range(chunks + LINE_LAG):
+        if turn < chunks:
+            j = turn
+            part = weight * lax.dot_general(
+                hidden, down_v[pl.ds(j * width, width), :], (((1,), (1,)), ((), ())),
+                preferred_element_type=jnp.float32,
+            )
+            core_out[j] = part[pair_rows:].astype(jnp.bfloat16)
+            back[j, "core"] = send(
+                core_out.at[j], core_in.at[j], r_send.at[j, 0], r_recv.at[j, 0], core_peer
+            )
+            kept_core[j] = part[:pair_rows]
+        if 0 <= turn - CORE_LAG < chunks:
+            j = turn - CORE_LAG
+            back[j, "core"].wait_recv()
+            part = kept_core[j, line_rows:] + core_in[j, line_rows:].astype(jnp.float32)
+            pair_out[j] = part.astype(jnp.bfloat16)
+            back[j, "pair"] = send(
+                pair_out.at[j], pair_in.at[j], r_send.at[j, line], r_recv.at[j, line], pair_peer
+            )
+            kept_pair[j] = kept_core[j, :line_rows] + core_in[j, :line_rows].astype(jnp.float32)
+        if 0 <= turn - PAIR_LAG < chunks:
+            j = turn - PAIR_LAG
+            back[j, "pair"].wait_recv()
+            part = kept_pair[j] + pair_in[j].astype(jnp.float32)
+            line_out[j] = part[height:].astype(jnp.bfloat16).reshape(line - 1, height, width)
+            for step in range(1, line):
+                back[j, step] = send(
+                    line_out.at[j, step - 1], line_in.at[j, step - 1],
+                    r_send.at[j, step], r_recv.at[j, step], line_peers[step - 1],
+                )
+            kept_line[j] = part[:height]
+        if 0 <= turn - LINE_LAG < chunks:
+            j = turn - LINE_LAG
+            total = kept_line[j]
+            for step in range(1, line):
+                back[j, step].wait_recv()
+                total += line_in[j, step - 1].astype(jnp.float32)
+            out[:, pl.ds(j * width, width)] = total.astype(out.dtype)
+    for copy in list(sent.values()) + list(back.values()):
+        copy.wait_send()
+
+
+def dense_device(tokens, expert_ids, route_weights, gate_weight, up_weight, down_weight):
+    height, feat_width = tokens.shape
+    units = gate_weight.shape[1]
+    n_expert = lax.axis_size("expert")
+    experts = n_expert // SPREAD
+    line = n_expert // 2
+    width = chunk_width(feat_width)
+    chunks = feat_width // width
+    total = 4 * line * height
+    bf16, f32 = jnp.bfloat16, jnp.float32
+    dma = pltpu.SemaphoreType.DMA
+    vmem, anywhere = pl.BlockSpec(memory_space=pltpu.VMEM), pl.BlockSpec(memory_space=pl.ANY)
+    return pl.pallas_call(
+        functools.partial(dense_kernel, experts),
+        out_shape=jax.ShapeDtypeStruct((height, feat_width), bf16),
+        in_specs=[anywhere, vmem, vmem, anywhere, anywhere, anywhere],
+        out_specs=vmem,
+        scratch_shapes=[
+            pltpu.VMEM((feat_width, units), bf16),
+            pltpu.VMEM((feat_width, units), bf16),
+            pltpu.VMEM((feat_width, units), bf16),
+            pltpu.VMEM((chunks, 2, 2, line, height, width), bf16),
+            pltpu.VMEM((2, 2, line, height, LANES), f32),
+            pltpu.VMEM((total, units), f32),
+            pltpu.VMEM((total, units), f32),
+            pltpu.VMEM((chunks, total // 2, width), f32),
+            pltpu.VMEM((chunks, total // 2, width), bf16),
+            pltpu.VMEM((chunks, total // 2, width), bf16),
+            pltpu.VMEM((chunks, total // 4, width), f32),
+            pltpu.VMEM((chunks, total // 4, width), bf16),
+            pltpu.VMEM((chunks, total // 4, width), bf16),
+            pltpu.VMEM((chunks, height, width), f32),
+            pltpu.VMEM((chunks, line - 1, height, width), bf16),
+            pltpu.VMEM((chunks, line - 1, height, width), bf16),
+            dma((3,)),
+            dma((chunks,)),
+            dma((chunks, line + 4)),
+            dma((chunks, line + 4)),
+            dma((line + 2,)),
+            dma((line + 2,)),
+            dma((chunks, line + 1)),
+            dma((chunks, line + 1)),
+        ],
+        compiler_params=pltpu.CompilerParams(
+            collective_id=0, has_side_effects=True, vmem_limit_bytes=40 * 1024 * 1024
+        ),
+        cost_estimate=pl.CostEstimate(
+            flops=6 * total * feat_width * units,
+            bytes_accessed=6 * feat_width * units,
+            transcendentals=total * units,
+        ),
+    )(tokens, expert_ids, route_weights, gate_weight, up_weight, down_weight)
+
+
 def solution(mesh):
     in_specs = (
         P(("groups", "expert", "cuts"), None),
@@ -90,6 +326,7 @@
         P(None, ("expert", "cuts")),
     )
     out_specs = P(("groups", "expert", "cuts"), None)
+    dense = mesh.shape["expert"] == CHOICES * SPREAD and mesh.shape["cuts"] == 2
     return jax.shard_map(
-        per_device, mesh=mesh, in_specs=in_specs, out_specs=out_specs, check_vma=False
-    )
+        dense_device if dense else per_device, mesh=mesh, in_specs=in_specs, out_specs=out_specs, check_vma=False
+    )

time: 134 us -> 55.6 us (0.41)
  waiting for transfers between devices: 61.1 us -> 0 us
  Pallas kernels: 0 us -> 47 us
  blocking collectives: 30.5 us -> 0 us
  between operations: 13.5 us -> 0.01 us
  matrix products: 11.8 us -> 0 us
  starting transfers between devices: 9.33 us -> 0 us
  local copies, waits for them, and re-layouts: 1.35 us -> 8.39 us
  other arithmetic: 6.37 us -> 0 us
    pallas_call x0 -> x1, Pallas kernels: none -> 47 us  [dense_device(): pl.pallas_call(functools.partial(dense_kernel, experts), out_shape=jax.Sh...]
    ppermute x2 -> x0, waiting for transfers between devices: 31.4 us -> none  [swapped(): return lax.ppermute(block, axis, route)]
    all_to_all x1 -> x0, blocking collectives: 30.5 us -> none  [per_device(): lax.all_to_all(copies, 'expert', split_axis=0, concat_axis=0, tiled=True)]
    reduce_scatter x1 -> x0, waiting for transfers between devices: 12.9 us -> none  [per_device(): lax.psum_scatter(partial_terms, 'cuts', scatter_dimension=0, tiled=True)]
    dot_general x4 -> x0, matrix products: 11.8 us -> none  [the longest x1 6.29 us: expert_part(): lax.dot_general(hidden, w_down, (((1,), (1,)), ((), ())), preferred_eleme...]
    all_gather x1 -> x0, waiting for transfers between devices: 8.93 us -> none  [per_device(): row_piece = lax.all_gather(arrived, 'cuts', axis=0, tiled=True)]
    all_to_all x1 -> x0, waiting for transfers between devices: 7.92 us -> none  [per_device(): lax.all_to_all(expert_rows, 'expert', split_axis=0, concat_axis=0, tiled=...]
    unnamed x6 -> x11, local copies, waits for them, and re-layouts: 0.94 us -> 8.39 us
  transfers between devices with their start and end apart: 5 -> 0, of which waited for: 5 -> 0; matrix products, arithmetic and copies ran while one was open for 0% -> 0% of each run, Pallas kernels for 0% -> 0%
where the time goes in v1:
time: 55.6 us; the launch traced here: 55.4 us
  Pallas kernels  47 us (85%)
  local copies, waits for them, and re-layouts  8.39 us (15%)
    pallas_call x1, Pallas kernels, dense_device(): pl.pallas_call(functools.partial(dense_kernel, experts), out_shape=jax.Sh...  47 us
    unnamed x11, local copies, waits for them, and re-layouts  8.39 us

profile of v1, /device:TPU:0, one launch (start us, length us, event | category | flops | bytes accessed | tf_op | source)
XLA Modules:
  0.0 55.4 jit_solution(8574637621787909767)
XLA Ops:
  0.0 0.8 %copy.7.ids = s32[16,2]{1,0:T(8,128)S(1)} copy(s32[16,2]{0,1:T(2,128)} %param.7) | data formatting | bytes 256 | tf_op args[1]
  0.8 0.8 %copy.8.mix = f32[16,2]{1,0:T(8,128)S(1)} copy(f32[16,2]{0,1:T(2,128)} %param.8) | data formatting | bytes 256 | tf_op args[2]
  1.5 0.0 copy-start
  1.5 1.8 %copy-done = bf16[3584,384]{1,0:T(8,128)(2,1)S(1)} copy-done((bf16[3584,384]{1,0:T(8,128)(2,1)S(1)}, bf16[3584,384]{1,0:T(8,128)(2,1)}, u32[]{:S(2)}) %copy-start) | copy-done | bytes 2752536
  3.3 0.0 copy-start.1
  3.3 1.8 %copy-done.1 = bf16[3584,384]{1,0:T(8,128)(2,1)S(1)} copy-done((bf16[3584,384]{1,0:T(8,128)(2,1)S(1)}, bf16[3584,384]{1,0:T(8,128)(2,1)}, u32[]{:S(2)}) %copy-start.1) | copy-done | bytes 2752536
  5.1 0.0 copy-start.2
  5.1 1.8 %copy-done.2 = bf16[3584,384]{1,0:T(8,128)(2,1)S(1)} copy-done((bf16[3584,384]{1,0:T(8,128)(2,1)S(1)}, bf16[3584,384]{1,0:T(8,128)(2,1)}, u32[]{:S(2)}) %copy-start.2) | copy-done | bytes 2752536
  6.8 0.0 copy-start.3
  6.8 0.9 %copy-done.3 = bf16[16,3584]{1,0:T(8,128)(2,1)S(1)} copy-done((bf16[16,3584]{1,0:T(8,128)(2,1)S(1)}, bf16[16,3584]{1,0:T(8,128)(2,1)}, u32[]{:S(2)}) %copy-start.3) | copy-done | bytes 114712
  7.7 47.0 %shard_map.64 = bf16[16,3584]{1,0:T(8,128)(2,1)S(1)} custom-call(bf16[16,3584]{1,0:T(8,128)(2,1)S(1)} %copy-done.3, s32[16,2]{1,0:T(8,128)S(1)} %copy.7.ids, f32[16,2]{1,0:T(8,128)S(1)} %copy.8.mix, bf16[3584,384]{1,0:T(8,128)(2,1)S(1)} %copy-done, bf16[3584,384]{1,0:T(8,128)(2,1)S(1)} %copy-done.1, bf16[3584,384]{1,0:T(8,128)(2,1)S(1)} %copy-done.2), custom_call_target="tpu_custom_call" | custom-call | flops 2113929216 | bytes 8257536 | tf_op jit(solution)/shard_map/pallas_call | solution.py:277
  54.7 0.6 %copy.10 = bf16[16,3584]{1,0:T(8,128)(2,1)} copy(bf16[16,3584]{1,0:T(8,128)(2,1)S(1)} %shard_map.64) | data formatting | bytes 229376
Async XLA Ops:
  1.5 1.8 %copy-start = (bf16[3584,384]{1,0:T(8,128)(2,1)S(1)}, bf16[3584,384]{1,0:T(8,128)(2,1)}, u32[]{:S(2)}) copy-start(bf16[3584,384]{1,0:T(8,128)(2,1)} %w_gate.1) | copy-start | bytes 8257540
  3.3 1.8 %copy-start.1 = (bf16[3584,384]{1,0:T(8,128)(2,1)S(1)}, bf16[3584,384]{1,0:T(8,128)(2,1)}, u32[]{:S(2)}) copy-start(bf16[3584,384]{1,0:T(8,128)(2,1)} %w_up.1) | copy-start | bytes 8257540
  5.1 1.8 %copy-start.2 = (bf16[3584,384]{1,0:T(8,128)(2,1)S(1)}, bf16[3584,384]{1,0:T(8,128)(2,1)}, u32[]{:S(2)}) copy-start(bf16[3584,384]{1,0:T(8,128)(2,1)} %w_down.1) | copy-start | bytes 8257540
  6.8 0.9 %copy-start.3 = (bf16[16,3584]{1,0:T(8,128)(2,1)S(1)}, bf16[16,3584]{1,0:T(8,128)(2,1)}, u32[]{:S(2)}) copy-start(bf16[16,3584]{1,0:T(8,128)(2,1)} %tok.1) | copy-start | bytes 344068

commit v2 on v1

--- a/solution.py
+++ b/solution.py
@@ -86,11 +86,12 @@
 
 CHOICES = 2
 LANES = 128
-CORE_LAG, PAIR_LAG, LINE_LAG = 1, 3, 5
-
-
-def chunk_width(feat_width):
-    for width in (512, 256, 128):
+CORE_LAG, PAIR_LAG, LINE_LAG = 1, 4, 7
+GATHER_WIDTHS, SCATTER_WIDTHS = (1792, 512, 256, 128), (512, 256, 128)
+
+
+def chunk_width(feat_width, widths):
+    for width in widths:
         if feat_width % width == 0:
             return width
     return feat_width
@@ -98,14 +99,16 @@
 
 def dense_kernel(
     experts, tok, ids, mix, w_gate, w_up, w_down, out,
-    gate_v, up_v, down_v, rows, scale, gate_acc, up_acc,
+    ids_v, mix_v, gate_v, up_v, down_v, rows, scale, gate_acc, up_acc,
     kept_core, core_out, core_in, kept_pair, pair_out, pair_in, kept_line, line_out, line_in,
-    w_sem, own_sem, g_send, g_recv, s_send, s_recv, r_send, r_recv,
+    w_sem, own_sem, up_send, down_send, line_recv, pair_send, pair_recv, core_send, core_recv, s_send, s_recv, r_send, r_recv,
 ):
     chunks, _, _, line, height, width = rows.shape
     n_expert = lax.axis_size("expert")
     place, core = lax.axis_index("expert"), lax.axis_index("cuts")
     along, side = place // 2, place % 2
+    up_peer = {"expert": lax.rem(along + 1, line) * 2 + side}
+    down_peer = {"expert": lax.rem(along + line - 1, line) * 2 + side}
     core_peer = {"cuts": 1 - core}
     pair_peer = {"expert": along * 2 + 1 - side}
     line_peers = [{"expert": lax.rem(along + step, line) * 2 + side} for step in range(1, line)]
@@ -120,14 +123,12 @@
         pltpu.make_async_copy(tok.at[:, pl.ds(j * width, width)], rows.at[j, 0, 0, 0], own_sem.at[j])
         for j in range(chunks)
     ]
-    for copy in own + loads:
+    small = [
+        pltpu.make_async_copy(ids, ids_v, w_sem.at[3]),
+        pltpu.make_async_copy(mix, mix_v, w_sem.at[4]),
+    ]
+    for copy in small + own + loads:
         copy.start()
-    lane = lax.broadcasted_iota(jnp.int32, (height, LANES), 1)
-    own_scale = jnp.zeros((height, LANES), jnp.float32)
-    for k in range(CHOICES):
-        own_scale += jnp.where(lane == ids[:, k:k + 1], mix[:, k:k + 1], 0.0)
-    scale[0, 0, 0] = own_scale
-
     barrier = pltpu.get_barrier_semaphore()
     for peer in peers:
         pl.semaphore_signal(barrier, inc=1, device_id=peer, device_id_type=pl.DeviceIdType.MESH)
@@ -141,73 +142,121 @@
         copy.start()
         return copy
 
+    def mine(j):
+        return tok.at[:, pl.ds(j * width, width)]
+
+    def to_line(j, step, upward):
+        held = line - step if upward else step
+        slot = line - step - 1 if upward else step + 1
+        return pltpu.make_async_remote_copy(
+            src_ref=mine(j) if step == 0 else rows.at[j, 0, 0, held],
+            dst_ref=rows.at[j, 0, 0, slot],
+            send_sem=(up_send if upward else down_send).at[j, step],
+            recv_sem=line_recv.at[j, slot],
+            device_id=up_peer if upward else down_peer,
+            device_id_type=pl.DeviceIdType.MESH,
+        )
+
+    def holds(step, upward):
+        return along >= step if upward else along <= line - 1 - step
+
+    def passes(step, upward):
+        return holds(step, upward) & (along < line - 1 if upward else along > 0)
+
+    def to_pair(j, slot):
+        return pltpu.make_async_remote_copy(
+            src_ref=mine(j) if slot == 0 else rows.at[j, 0, 0, slot],
+            dst_ref=rows.at[j, 0, 1, slot],
+            send_sem=pair_send.at[j, slot], recv_sem=pair_recv.at[j, slot],
+            device_id=pair_peer, device_id_type=pl.DeviceIdType.MESH,
+        )
+
+    def to_core(j, row, slot):
+        return pltpu.make_async_remote_copy(
+            src_ref=mine(j) if (row, slot) == (0, 0) else rows.at[j, 0, row, slot],
+            dst_ref=rows.at[j, 1, row, slot],
+            send_sem=core_send.at[j, row, slot], recv_sem=core_recv.at[j, row, slot],
+            device_id=core_peer, device_id_type=pl.DeviceIdType.MESH,
+        )
+
+    for j in range(chunks):
+        for upward in (True, False):
+            pl.when(passes(0, upward))(lambda j=j, upward=upward: to_line(j, 0, upward).start())
+        to_pair(j, 0).start()
+    for j in range(chunks):
+        to_core(j, 0, 0).start()
+    for copy in small:
+        copy.wait()
+    diagonal = lax.broadcasted_iota(jnp.int32, (height, height), 0) == lax.broadcasted_iota(
+        jnp.int32, (height, height), 1
+    )
+    lane = lax.broadcasted_iota(jnp.int32, (height, LANES), 1)
+    own_scale = jnp.zeros((height, LANES), jnp.float32)
+    for k in range(CHOICES):
+        name = jnp.sum(jnp.where(diagonal, ids_v[k:k + 1, :], 0), axis=1, keepdims=True)
+        share = jnp.sum(jnp.where(diagonal, mix_v[k:k + 1, :], 0.0), axis=1, keepdims=True)
+        own_scale += jnp.where(lane == name, share, 0.0)
+    scale[0, 0, 0] = own_scale
     sent = {}
-    for j in range(chunks):
-        mine = tok.at[:, pl.ds(j * width, width)]
-        for step in range(1, line):
-            sent[j, step] = send(
-                mine, rows.at[j, 0, 0, line - step], g_send.at[j, step], g_recv.at[j, line - step],
-                line_peers[step - 1],
-            )
-        sent[j, "pair own"] = send(
-            mine, rows.at[j, 0, 1, 0], g_send.at[j, line], g_recv.at[j, line], pair_peer
-        )
     for step in range(1, line):
         sent["s", step] = send(
             scale.at[0, 0, 0], scale.at[0, 0, line - step], s_send.at[step], s_recv.at[line - step],
             line_peers[step - 1],
         )
 
-    for turn in range(chunks + 2):
-        if turn < chunks:
-            j = turn
-            for step in range(1, line):
-                sent[j, line - step].wait_recv()
-            sent[j, "pair"] = send(
-                rows.at[j, 0, 0, pl.ds(1, line - 1)], rows.at[j, 0, 1, pl.ds(1, line - 1)],
-                g_send.at[j, line + 1], g_recv.at[j, line + 1], pair_peer,
-            )
-            own[j].wait()
-            sent[j, "core"] = send(
-                rows.at[j, 0, 0], rows.at[j, 1, 0],
-                g_send.at[j, line + 2], g_recv.at[j, line + 2], core_peer,
-            )
-        if turn == chunks - 1:
-            for step in range(1, line):
-                sent["s", line - step].wait_recv()
+    def line_arrival(j, step, upward):
+        slot = line - step if upward else step
+        to_line(j, step - 1, upward).wait_recv()
+        if step < line - 1:
+            pl.when(passes(step, upward))(lambda: to_line(j, step, upward).start())
+        to_pair(j, slot).start()
+        to_core(j, 0, slot).start()
+
+    def pair_arrival(j, slot):
+        to_pair(j, slot).wait_recv()
+        to_core(j, 1, slot).start()
+
+    for step in range(1, line + 1):
+        for j in range(chunks):
+            if step < line:
+                for upward in (True, False):
+                    pl.when(holds(step, upward))(
+                        lambda j=j, step=step, upward=upward: line_arrival(j, step, upward)
+                    )
+            if step == 1:
+                pair_arrival(j, 0)
+            else:
+                for upward in (True, False):
+                    slot = line - step + 1 if upward else step - 1
+                    pl.when(holds(step - 1, upward))(lambda j=j, slot=slot: pair_arrival(j, slot))
+        if step == line - 2:
+            for hop in range(1, line):
+                sent["s", line - hop].wait_recv()
             sent["s", "pair"] = send(
                 scale.at[0, 0], scale.at[0, 1], s_send.at[line], s_recv.at[line], pair_peer
             )
-        if 1 <= turn <= chunks:
-            j = turn - 1
-            sent[j, "pair own"].wait_recv()
-            sent[j, "pair"].wait_recv()
-            sent[j, "core pair"] = send(
-                rows.at[j, 0, 1], rows.at[j, 1, 1],
-                g_send.at[j, line + 3], g_recv.at[j, line + 3], core_peer,
-            )
-        if turn == chunks:
+        if step == line - 1:
             sent["s", "pair"].wait_recv()
             sent["s", "core"] = send(
                 scale.at[0], scale.at[1], s_send.at[line + 1], s_recv.at[line + 1], core_peer
             )
-        if turn >= 2:
-            j = turn - 2
-            sent[j, "core"].wait_recv()
-            sent[j, "core pair"].wait_recv()
-            if j == 0:
-                loads[0].wait()
-                loads[1].wait()
-            block = rows[j].reshape(-1, width)
-            depth = pl.ds(j * width, width)
-            gate_part = jnp.dot(block, gate_v[depth, :], preferred_element_type=jnp.float32)
-            up_part = jnp.dot(block, up_v[depth, :], preferred_element_type=jnp.float32)
-            if j == 0:
-                gate_acc[...] = gate_part
-                up_acc[...] = up_part
-            else:
-                gate_acc[...] += gate_part
-                up_acc[...] += up_part
+    loads[0].wait()
+    loads[1].wait()
+    for j in range(chunks):
+        own[j].wait()
+        for row in range(2):
+            for slot in range(line):
+                to_core(j, row, slot).wait_recv()
+        block = rows[j].reshape(-1, width)
+        depth = pl.ds(j * width, width)
+        gate_part = jnp.dot(block, gate_v[depth, :], preferred_element_type=jnp.float32)
+        up_part = jnp.dot(block, up_v[depth, :], preferred_element_type=jnp.float32)
+        if j == 0:
+            gate_acc[...] = gate_part
+            up_acc[...] = up_part
+        else:
+            gate_acc[...] += gate_part
+            up_acc[...] += up_part
 
     gate = gate_acc[...]
     hidden = (gate / (1.0 + jnp.exp(-gate)) * up_acc[...]).astype(jnp.bfloat16)
@@ -217,13 +266,14 @@
     weight = jnp.sum(jnp.where(lane == my_expert, weights, 0.0), axis=1, keepdims=True)
     loads[2].wait()
 
+    parts, _, span = core_out.shape
     pair_rows, line_rows = 2 * line * height, line * height
     back = {}
-    for turn in range(chunks + LINE_LAG):
-        if turn < chunks:
+    for turn in range(parts + LINE_LAG):
+        if turn < parts:
             j = turn
             part = weight * lax.dot_general(
-                hidden, down_v[pl.ds(j * width, width), :], (((1,), (1,)), ((), ())),
+                hidden, down_v[pl.ds(j * span, span), :], (((1,), (1,)), ((), ())),
                 preferred_element_type=jnp.float32,
             )
             core_out[j] = part[pair_rows:].astype(jnp.bfloat16)
@@ -231,7 +281,7 @@
                 core_out.at[j], core_in.at[j], r_send.at[j, 0], r_recv.at[j, 0], core_peer
             )
             kept_core[j] = part[:pair_rows]
-        if 0 <= turn - CORE_LAG < chunks:
+        if 0 <= turn - CORE_LAG < parts:
             j = turn - CORE_LAG
             back[j, "core"].wait_recv()
             part = kept_core[j, line_rows:] + core_in[j, line_rows:].astype(jnp.float32)
@@ -240,24 +290,34 @@
                 pair_out.at[j], pair_in.at[j], r_send.at[j, line], r_recv.at[j, line], pair_peer
             )
             kept_pair[j] = kept_core[j, :line_rows] + core_in[j, :line_rows].astype(jnp.float32)
-        if 0 <= turn - PAIR_LAG < chunks:
+        if 0 <= turn - PAIR_LAG < parts:
             j = turn - PAIR_LAG
             back[j, "pair"].wait_recv()
             part = kept_pair[j] + pair_in[j].astype(jnp.float32)
-            line_out[j] = part[height:].astype(jnp.bfloat16).reshape(line - 1, height, width)
+            line_out[j] = part[height:].astype(jnp.bfloat16).reshape(line - 1, height, span)
             for step in range(1, line):
                 back[j, step] = send(
                     line_out.at[j, step - 1], line_in.at[j, step - 1],
                     r_send.at[j, step], r_recv.at[j, step], line_peers[step - 1],
                 )
             kept_line[j] = part[:height]
-        if 0 <= turn - LINE_LAG < chunks:
+        if 0 <= turn - LINE_LAG < parts:
             j = turn - LINE_LAG
             total = kept_line[j]
             for step in range(1, line):
                 back[j, step].wait_recv()
                 total += line_in[j, step - 1].astype(jnp.float32)
-            out[:, pl.ds(j * width, width)] = total.astype(out.dtype)
+            out[:, pl.ds(j * span, span)] = total.astype(out.dtype)
+    for j in range(chunks):
+        for step in range(line - 1):
+            for upward in (True, False):
+                pl.when(passes(step, upward))(
+                    lambda j=j, step=step, upward=upward: to_line(j, step, upward).wait_send()
+                )
+        for slot in range(line):
+            to_pair(j, slot).wait_send()
+            for row in range(2):
+                to_core(j, row, slot).wait_send()
     for copy in list(sent.values()) + list(back.values()):
         copy.wait_send()
 
@@ -268,18 +328,20 @@
     n_expert = lax.axis_size("expert")
     experts = n_expert // SPREAD
     line = n_expert // 2
-    width = chunk_width(feat_width)
-    chunks = feat_width // width
+    width, span = chunk_width(feat_width, GATHER_WIDTHS), chunk_width(feat_width, SCATTER_WIDTHS)
+    chunks, parts = feat_width // width, feat_width // span
     total = 4 * line * height
     bf16, f32 = jnp.bfloat16, jnp.float32
     dma = pltpu.SemaphoreType.DMA
-    vmem, anywhere = pl.BlockSpec(memory_space=pltpu.VMEM), pl.BlockSpec(memory_space=pl.ANY)
+    vmem, hbm = pl.BlockSpec(memory_space=pltpu.VMEM), pl.BlockSpec(memory_space=pltpu.HBM)
     return pl.pallas_call(
         functools.partial(dense_kernel, experts),
         out_shape=jax.ShapeDtypeStruct((height, feat_width), bf16),
-        in_specs=[anywhere, vmem, vmem, anywhere, anywhere, anywhere],
+        in_specs=[hbm] * 6,
         out_specs=vmem,
         scratch_shapes=[
+            pltpu.VMEM((CHOICES, height), jnp.int32),
+            pltpu.VMEM((CHOICES, height), f32),
             pltpu.VMEM((feat_width, units), bf16),
             pltpu.VMEM((feat_width, units), bf16),
             pltpu.VMEM((feat_width, units), bf16),
@@ -287,33 +349,38 @@
             pltpu.VMEM((2, 2, line, height, LANES), f32),
             pltpu.VMEM((total, units), f32),
             pltpu.VMEM((total, units), f32),
-            pltpu.VMEM((chunks, total // 2, width), f32),
-            pltpu.VMEM((chunks, total // 2, width), bf16),
-            pltpu.VMEM((chunks, total // 2, width), bf16),
-            pltpu.VMEM((chunks, total // 4, width), f32),
-            pltpu.VMEM((chunks, total // 4, width), bf16),
-            pltpu.VMEM((chunks, total // 4, width), bf16),
-            pltpu.VMEM((chunks, height, width), f32),
-            pltpu.VMEM((chunks, line - 1, height, width), bf16),
-            pltpu.VMEM((chunks, line - 1, height, width), bf16),
-            dma((3,)),
+            pltpu.VMEM((parts, total // 2, span), f32),
+            pltpu.VMEM((parts, total // 2, span), bf16),
+            pltpu.VMEM((parts, total // 2, span), bf16),
+            pltpu.VMEM((parts, total // 4, span), f32),
+            pltpu.VMEM((parts, total // 4, span), bf16),
+            pltpu.VMEM((parts, total // 4, span), bf16),
+            pltpu.VMEM((parts, height, span), f32),
+            pltpu.VMEM((parts, line - 1, height, span), bf16),
+            pltpu.VMEM((parts, line - 1, height, span), bf16),
+            dma((5,)),
             dma((chunks,)),
-            dma((chunks, line + 4)),
-            dma((chunks, line + 4)),
+            dma((chunks, line)),
+            dma((chunks, line)),
+            dma((chunks, line)),
+            dma((chunks, line)),
+            dma((chunks, line)),
+            dma((chunks, 2, line)),
+            dma((chunks, 2, line)),
             dma((line + 2,)),
             dma((line + 2,)),
-            dma((chunks, line + 1)),
-            dma((chunks, line + 1)),
+            dma((parts, line + 1)),
+            dma((parts, line + 1)),
         ],
         compiler_params=pltpu.CompilerParams(
-            collective_id=0, has_side_effects=True, vmem_limit_bytes=40 * 1024 * 1024
+            collective_id=0, has_side_effects=True, vmem_limit_bytes=64000000
         ),
         cost_estimate=pl.CostEstimate(
             flops=6 * total * feat_width * units,
             bytes_accessed=6 * feat_width * units,
             transcendentals=total * units,
         ),
-    )(tokens, expert_ids, route_weights, gate_weight, up_weight, down_weight)
+    )(tokens, expert_ids.T, route_weights.T, gate_weight, up_weight, down_weight)
 
 
 def solution(mesh):

time: 55.6 us -> 43.3 us (0.78)
  local copies, waits for them, and re-layouts: 8.39 us -> 1.55 us
  Pallas kernels: 47 us -> 41.6 us
    unnamed x11 -> x1, local copies, waits for them, and re-layouts: 8.39 us -> 1.55 us
    pallas_call x1, Pallas kernels: 47 us -> 41.6 us  [dense_device(): pl.pallas_call(functools.partial(dense_kernel, experts), out_shape=jax.Sh...]
where the time goes in v2:
time: 43.3 us; the launch traced here: 43.2 us
  Pallas kernels  41.6 us (96%)
  local copies, waits for them, and re-layouts  1.55 us (4%)
    pallas_call x1, Pallas kernels, dense_device(): pl.pallas_call(functools.partial(dense_kernel, experts), out_shape=jax.Sh...  41.6 us
    unnamed x1, local copies, waits for them, and re-layouts  1.55 us

profile of v2, /device:TPU:0, one launch (start us, length us, event | category | flops | bytes accessed | tf_op | source)
XLA Modules:
  0.0 43.2 jit_solution(13649601839009938452)
XLA Ops:
  0.0 41.6 %shard_map.64 = bf16[16,3584]{1,0:T(8,128)(2,1)} custom-call(bf16[16,3584]{1,0:T(8,128)(2,1)} %tok.1, s32[2,16]{1,0:T(2,128)} %bitcast.2, f32[2,16]{1,0:T(2,128)} %bitcast.3, bf16[3584,384]{1,0:T(8,128)(2,1)} %w_gate.1, bf16[3584,384]{1,0:T(8,128)(2,1)} %w_up.1, bf16[3584,384]{1,0:T(8,128)(2,1)} %w_down.1), custom_call_target="tpu_custom_call" | custom-call | flops 2113929216 | bytes 8257536 | tf_op jit(solution)/shard_map/pallas_call | solution.py:337
  41.6 1.6 %copy.8 = bf16[16,3584]{1,0:T(8,128)(2,1)} copy(bf16[16,3584]{1,0:T(8,128)(2,1)} %shard_map.64) | data formatting | bytes 229376

commit v3 on v2

--- a/solution.py
+++ b/solution.py
@@ -87,6 +87,7 @@
 CHOICES = 2
 LANES = 128
 CORE_LAG, PAIR_LAG, LINE_LAG = 1, 4, 7
+GATHER_LAG = 2
 GATHER_WIDTHS, SCATTER_WIDTHS = (1792, 512, 256, 128), (512, 256, 128)
 
 
@@ -101,7 +102,7 @@
     experts, tok, ids, mix, w_gate, w_up, w_down, out,
     ids_v, mix_v, gate_v, up_v, down_v, rows, scale, gate_acc, up_acc,
     kept_core, core_out, core_in, kept_pair, pair_out, pair_in, kept_line, line_out, line_in,
-    w_sem, own_sem, up_send, down_send, line_recv, pair_send, pair_recv, core_send, core_recv, s_send, s_recv, r_send, r_recv,
+    w_sem, own_sem, up_send, down_send, line_recv, pair_send, pair_recv, core_send, core_recv, s_send, s_recv, r_send, r_recv, mixed, out_sem,
 ):
     chunks, _, _, line, height, width = rows.shape
     n_expert = lax.axis_size("expert")
@@ -216,26 +217,28 @@
         to_pair(j, slot).wait_recv()
         to_core(j, 1, slot).start()
 
-    for step in range(1, line + 1):
+    for turn in range(1, line + GATHER_LAG):
+        if turn < line:
+            for j in range(chunks):
+                for upward in (True, False):
+                    pl.when(holds(turn, upward))(
+                        lambda j=j, step=turn, upward=upward: line_arrival(j, step, upward)
+                    )
+        step = turn - GATHER_LAG
         for j in range(chunks):
-            if step < line:
+            if step == 0:
+                pair_arrival(j, 0)
+            elif step > 0:
                 for upward in (True, False):
-                    pl.when(holds(step, upward))(
-                        lambda j=j, step=step, upward=upward: line_arrival(j, step, upward)
-                    )
-            if step == 1:
-                pair_arrival(j, 0)
-            else:
-                for upward in (True, False):
-                    slot = line - step + 1 if upward else step - 1
-                    pl.when(holds(step - 1, upward))(lambda j=j, slot=slot: pair_arrival(j, slot))
-        if step == line - 2:
+                    slot = line - step if upward else step
+                    pl.when(holds(step, upward))(lambda j=j, slot=slot: pair_arrival(j, slot))
+        if turn == line - 1:
             for hop in range(1, line):
                 sent["s", line - hop].wait_recv()
             sent["s", "pair"] = send(
                 scale.at[0, 0], scale.at[0, 1], s_send.at[line], s_recv.at[line], pair_peer
             )
-        if step == line - 1:
+        if turn == line:
             sent["s", "pair"].wait_recv()
             sent["s", "core"] = send(
                 scale.at[0], scale.at[1], s_send.at[line + 1], s_recv.at[line + 1], core_peer
@@ -307,7 +310,11 @@
             for step in range(1, line):
                 back[j, step].wait_recv()
                 total += line_in[j, step - 1].astype(jnp.float32)
-            out[:, pl.ds(j * span, span)] = total.astype(out.dtype)
+            mixed[j] = total.astype(mixed.dtype)
+            back[j, "out"] = pltpu.make_async_copy(
+                mixed.at[j], out.at[:, pl.ds(j * span, span)], out_sem.at[j]
+            )
+            back[j, "out"].start()
     for j in range(chunks):
         for step in range(line - 1):
             for upward in (True, False):
@@ -318,8 +325,11 @@
             to_pair(j, slot).wait_send()
             for row in range(2):
                 to_core(j, row, slot).wait_send()
-    for copy in list(sent.values()) + list(back.values()):
-        copy.wait_send()
+    for key, copy in list(sent.items()) + list(back.items()):
+        if key[1] == "out":
+            copy.wait()
+        else:
+            copy.wait_send()
 
 
 def dense_device(tokens, expert_ids, route_weights, gate_weight, up_weight, down_weight):
@@ -333,12 +343,12 @@
     total = 4 * line * height
     bf16, f32 = jnp.bfloat16, jnp.float32
     dma = pltpu.SemaphoreType.DMA
-    vmem, hbm = pl.BlockSpec(memory_space=pltpu.VMEM), pl.BlockSpec(memory_space=pltpu.HBM)
+    hbm = pl.BlockSpec(memory_space=pltpu.HBM)
     return pl.pallas_call(
         functools.partial(dense_kernel, experts),
         out_shape=jax.ShapeDtypeStruct((height, feat_width), bf16),
         in_specs=[hbm] * 6,
-        out_specs=vmem,
+        out_specs=hbm,
         scratch_shapes=[
             pltpu.VMEM((CHOICES, height), jnp.int32),
             pltpu.VMEM((CHOICES, height), f32),
@@ -371,6 +381,8 @@
             dma((line + 2,)),
             dma((parts, line + 1)),
             dma((parts, line + 1)),
+            pltpu.VMEM((parts, height, span), bf16),
+            dma((parts,)),
         ],
         compiler_params=pltpu.CompilerParams(
             collective_id=0, has_side_effects=True, vmem_limit_bytes=64000000

time: 43.3 us -> 42.8 us (0.988)
  Pallas kernels: 41.6 us -> 41.1 us
    pallas_call x1, Pallas kernels: 41.6 us -> 41.1 us  [dense_device(): pl.pallas_call(functools.partial(dense_kernel, experts), out_shape=jax.Sh...]
where the time goes in v3:
time: 42.8 us; the launch traced here: 42.7 us
  Pallas kernels  41.1 us (96%)
  local copies, waits for them, and re-layouts  1.55 us (4%)
    pallas_call x1, Pallas kernels, dense_device(): pl.pallas_call(functools.partial(dense_kernel, experts), out_shape=jax.Sh...  41.1 us
    unnamed x1, local copies, waits for them, and re-layouts  1.55 us

profile of v3, /device:TPU:0, one launch (start us, length us, event | category | flops | bytes accessed | tf_op | source)
XLA Modules:
  0.0 42.7 jit_solution(6685693112720456375)
XLA Ops:
  0.0 41.1 %shard_map.64 = bf16[16,3584]{1,0:T(8,128)(2,1)} custom-call(bf16[16,3584]{1,0:T(8,128)(2,1)} %tok.1, s32[2,16]{1,0:T(2,128)} %bitcast.2, f32[2,16]{1,0:T(2,128)} %bitcast.3, bf16[3584,384]{1,0:T(8,128)(2,1)} %w_gate.1, bf16[3584,384]{1,0:T(8,128)(2,1)} %w_up.1, bf16[3584,384]{1,0:T(8,128)(2,1)} %w_down.1), custom_call_target="tpu_custom_call" | custom-call | flops 2113929216 | bytes 8257536 | tf_op jit(solution)/shard_map/pallas_call | solution.py:347
  41.1 1.6 %copy.8 = bf16[16,3584]{1,0:T(8,128)(2,1)} copy(bf16[16,3584]{1,0:T(8,128)(2,1)} %shard_map.64) | data formatting | bytes 229376
